TPU v7x, 32 devices: a whole 2x2x4 slice. The times are simulated.
32 devices in a mesh: wave: 16 (over z, y, x), lev: 2 (over core).
Axes of the slice: x: 2, y: 2, z: 4, core: 2. Of those that a mesh axis runs over, the one named last changes fastest.
Arguments:
- fourier_in: bfloat16 [3, 28, 1280, 64], P(None, 'lev', 'wave'), may hold values from -6 to 6
- spectral_old: bfloat16 [3, 28, 16, 2816], P(None, 'lev', 'wave'), may hold values from -6 to 6
- legendre: bfloat16 [16, 1408, 1280], P('wave'), may hold values from -0.15625 to 0.15625
- g_matrix: float32 [28, 28], replicated, may hold values from -1 to 1
- modes_in: float32 [28, 28], replicated, may hold values from -1 to 1
- modes_out: float32 [28, 28], replicated, may hold values from -1 to 1
- mode_heating: float32 [28, 28], replicated, may hold values from -1 to 1
- mode_rates: float32 [28], replicated, may hold values from 0.1 to 10
- pair_ids: int32 [16], replicated, may hold values from 0 to 639, as said below
- lat_ids: int32 [1280], replicated, may hold values from 0 to 1279, each once
- limits: int32 [1280], replicated, may hold values from 10 to 1280
Outputs:
- spectral_new: bfloat16 [3, 28, 16, 2816], P(None, 'lev', 'wave')
- fourier_out: bfloat16 [3, 28, 1280, 64], P(None, 'lev', 'wave')
Inputs may be any that keep to these rules, and one draw needn't show every extreme that they name: `pair_ids`: distinct pair numbers. `lat_ids`: each latitude once.
All inputs are finite; a program needn't handle non-finite values.
Results may differ from a plain program's by a relative error of at most 0.018.
Values may be sent and summed in bfloat16 or wider, within the bound.
A program may use at most 64 MiB of HBM per device.

v0:
```python
import jax
import jax.numpy as jnp
from jax import lax
from jax.sharding import PartitionSpec as P

MMAX = 1280
BLOCK = 64
coupling = 2.0
highest = lax.Precision.HIGHEST


def pair_layout(pair_number, row_count):
    row_index = jnp.arange(row_count, dtype=jnp.int32)
    first_length = MMAX - pair_number
    first_pad = (first_length + BLOCK - 1) // BLOCK * BLOCK
    in_first = row_index < first_pad
    row_valid = jnp.where(
        in_first, row_index < first_length, row_index - first_pad < pair_number + 1
    )
    degree = jnp.where(
        in_first, pair_number + row_index, MMAX - 1 - pair_number + row_index - first_pad
    ).astype(jnp.float32)
    lfactor = degree * (degree + 1.0) / float(MMAX * (MMAX - 1))
    return (row_valid, lfactor, first_pad)


def level_term(matrix, vector, level_start, lev_count, row_start, row_total):
    rows_block = lax.dynamic_slice(
        matrix, (jnp.asarray(row_start, jnp.int32), level_start), (row_total, lev_count)
    )
    return jnp.dot(rows_block, vector, precision=highest, preferred_element_type=jnp.float32)


def legendre_forward(stacked, pair_table, first_pad, pair_number, row_count):
    column_count = stacked.shape[1]

    def block_step(block_index, running, which_wave):
        start_row = block_index * BLOCK
        table_rows = lax.dynamic_slice_in_dim(pair_table, start_row, BLOCK, 0)
        product = lax.dot_general(
            stacked[which_wave],
            table_rows,
            (((1,), (1,)), ((), ())),
            preferred_element_type=jnp.float32,
        )
        return lax.dynamic_update_slice_in_dim(running, product, start_row, 1)

    running = jnp.zeros((column_count, row_count), jnp.float32)
    split_block = first_pad // BLOCK
    end_block = (first_pad + pair_number + BLOCK) // BLOCK
    running = lax.fori_loop(
        0, split_block, lambda block_index, carried: block_step(block_index, carried, 0), running
    )
    running = lax.fori_loop(
        split_block,
        end_block,
        lambda block_index, carried: block_step(block_index, carried, 1),
        running,
    )
    return running


def legendre_inverse(slot_spectra, pair_table, first_pad, pair_number):
    column_count = slot_spectra.shape[0]
    lat_total = pair_table.shape[1]

    def block_step(block_index, running):
        start_row = block_index * BLOCK
        table_rows = lax.dynamic_slice_in_dim(pair_table, start_row, BLOCK, 0)
        spectra_rows = lax.dynamic_slice_in_dim(slot_spectra, start_row, BLOCK, 1)
        return running + jnp.dot(spectra_rows, table_rows, preferred_element_type=jnp.float32)

    zeros_grid = jnp.zeros((column_count, lat_total), jnp.float32)
    split_block = first_pad // BLOCK
    end_block = (first_pad + pair_number + BLOCK) // BLOCK
    first_wave = lax.fori_loop(0, split_block, block_step, zeros_grid)
    second_wave = lax.fori_loop(split_block, end_block, block_step, zeros_grid)
    return jnp.stack([first_wave, second_wave])


def body(
    fourier_in,
    spectral_old,
    legendre,
    g_matrix,
    modes_in,
    modes_out,
    mode_heating,
    mode_rates,
    pair_ids,
    lat_ids,
    limits,
):
    lev_count = fourier_in.shape[1]
    lat_count = fourier_in.shape[2]
    pair_count = legendre.shape[0]
    row_count = legendre.shape[1]
    lat_total = legendre.shape[2]
    wave_index = lax.axis_index("wave")
    level_start = lax.axis_index("lev") * lev_count
    pair_slot = 0
    pair_number = lax.dynamic_slice_in_dim(pair_ids, wave_index * pair_count + pair_slot, 1)[0]
    layouts = [(pair_number,) + pair_layout(pair_number, row_count)]
    own_lats = lax.dynamic_slice_in_dim(lat_ids, wave_index * lat_count, lat_count)
    matches = own_lats[:, None] == jnp.arange(lat_total, dtype=jnp.int32)[None, :]
    row_limit = jnp.sum(jnp.where(matches, limits[None, :], 0), axis=1)
    both_waves = jnp.stack([pair_ids, MMAX - 1 - pair_ids], axis=1)
    column_wave = jnp.repeat(both_waves, 2, axis=1).reshape(-1)
    keep_mask = column_wave[None, :] < row_limit[:, None]
    masked = jnp.where(keep_mask[None, None], fourier_in, jnp.zeros((), fourier_in.dtype))
    exchanged = lax.all_to_all(masked, "wave", split_axis=3, concat_axis=2, tiled=True)
    item_count = exchanged.shape[0]
    column_count = item_count * lev_count * 2
    pair_slot = 0
    pair_number, row_valid, lfactor, first_pad = layouts[pair_slot]
    slot_data = exchanged.reshape(item_count, lev_count, lat_total, 2, 2)
    stacked = jnp.transpose(slot_data, (3, 0, 1, 4, 2)).reshape(2, column_count, lat_total)
    spectra = legendre_forward(stacked, legendre[pair_slot], first_pad, pair_number, row_count)
    spectra = jnp.where(row_valid[None, :], spectra, 0.0)
    results = [spectra.reshape(item_count, lev_count, 2, row_count)]
    tendency = jnp.stack(results, axis=2)
    flat_size = pair_count * 2 * row_count
    old_fields = spectral_old.reshape(3, lev_count, pair_count, 2, row_count).astype(jnp.float32)
    vorticity = (old_fields[0] + tendency[0]).reshape(lev_count, flat_size)
    divergence = (old_fields[1] + tendency[1]).reshape(lev_count, flat_size)
    heat_star = (old_fields[2] + tendency[2]).reshape(lev_count, flat_size)
    wave_factor = jnp.stack(
        [jnp.broadcast_to(layout[2][None, :], (2, row_count)) for layout in layouts]
    ).reshape(1, flat_size)
    keep_rows = jnp.stack(
        [jnp.broadcast_to(layout[1][None, :], (2, row_count)) for layout in layouts]
    ).reshape(1, flat_size)
    rates_own = lax.dynamic_slice_in_dim(mode_rates, level_start, lev_count)
    hydrostatic = lax.psum_scatter(
        level_term(
            g_matrix,
            heat_star,
            level_start,
            lev_count,
            jnp.int32(0),
            lev_count * lax.axis_size("lev"),
        ).astype(jnp.bfloat16),
        "lev",
        scatter_dimension=0,
        tiled=True,
    ).astype(jnp.float32)
    right_own = divergence + coupling * wave_factor * hydrostatic
    projected = lax.psum_scatter(
        level_term(
            modes_in,
            right_own,
            level_start,
            lev_count,
            jnp.int32(0),
            lev_count * lax.axis_size("lev"),
        ).astype(jnp.bfloat16),
        "lev",
        scatter_dimension=0,
        tiled=True,
    ).astype(jnp.float32)
    modal_part = projected / (1.0 + coupling * coupling * wave_factor * rates_own[:, None])
    row_start = jnp.int32(0)
    row_total = lev_count * lax.axis_size("lev")
    divergence_part = level_term(
        modes_out, modal_part, level_start, lev_count, row_start, row_total
    )
    heating_part = level_term(
        mode_heating, modal_part, level_start, lev_count, row_start, row_total
    )
    rebuilt = lax.psum_scatter(
        jnp.stack([divergence_part, heating_part], axis=1).astype(jnp.bfloat16),
        "lev",
        scatter_dimension=0,
        tiled=True,
    ).astype(jnp.float32)
    vorticity_out = jnp.where(keep_rows, vorticity, 0.0).astype(jnp.bfloat16)
    divergence_out = jnp.where(keep_rows, rebuilt[:, 0], 0.0).astype(jnp.bfloat16)
    heat_out = jnp.where(keep_rows, heat_star - coupling * rebuilt[:, 1], 0.0).astype(jnp.bfloat16)
    spectral_new = jnp.stack([vorticity_out, divergence_out, heat_out]).reshape(
        3, lev_count, pair_count, 2 * row_count
    )
    pair_slot = 0
    pair_number, row_valid, lfactor, first_pad = layouts[pair_slot]
    slot_spectra = spectral_new[:, :, pair_slot].reshape(3 * lev_count * 2, row_count)
    grid_part = legendre_inverse(slot_spectra, legendre[pair_slot], first_pad, pair_number)
    grid_part = (
        grid_part.reshape(2, 3, lev_count, 2, lat_total)
        .transpose(1, 2, 4, 0, 3)
        .reshape(3, lev_count, lat_total, 4)
    )
    gridded = grid_part.astype(jnp.bfloat16)
    returned = lax.all_to_all(gridded, "wave", split_axis=2, concat_axis=3, tiled=True)
    fourier_out = jnp.where(keep_mask[None, None], returned, jnp.zeros((), jnp.bfloat16))
    return (spectral_new, fourier_out)


def solution(mesh):
    placed = (
        P(None, "lev", "wave", None),
        P(None, "lev", "wave", None),
        P("wave", None, None),
        P(),
        P(),
        P(),
        P(),
        P(),
        P(),
        P(),
        P(),
    )
    return jax.shard_map(
        body,
        mesh=mesh,
        in_specs=placed,
        out_specs=(P(None, "lev", "wave", None), P(None, "lev", "wave", None)),
        check_vma=False,
    )
```

profile of v0, /device:TPU:0, one launch (start us, length us, event | category | flops | bytes accessed | tf_op | source)
XLA Modules:
  0.0 189.5 jit_solution(12464096708221175484)
XLA Ops:
  11.8 1.3 copy.81
  13.1 8.3 %all-to-all-start = ((bf16[3,14,80,64]{2,1,0,3:T(8,128)(2,1)}), bf16[3,14,80,64]{2,1,0,3:T(8,128)(2,1)S(1)}, u32[]{:S(2)}, u32[]{:S(2)}) async-start(bf16[3,14,80,64]{2,1,0,3:T(8,128)(2,1)} %copy.81), calls=%async_computation | async-start | bytes 1572864 | tf_op jit(solution)/shard_map/all_to_all | solution.py:111
  25.5 15.7 %all-to-all-done = bf16[3,14,80,64]{2,1,0,3:T(8,128)(2,1)S(1)} async-done(((bf16[3,14,80,64]{2,1,0,3:T(8,128)(2,1)}), bf16[3,14,80,64]{2,1,0,3:T(8,128)(2,1)S(1)}, u32[]{:S(2)}, u32[]{:S(2)}) %all-to-all-start) | async-done | bytes 430112 | tf_op jit(solution)/shard_map/all_to_all | solution.py:111
  43.2 19.2 %while.40 = (s32[]{:T(128)}, f32[84,1408]{0,1:T(8,128)S(1)}, s32[]{:T(128)}, bf16[1408,1280]{1,0:T(8,128)(2,1)}, bf16[2,84,1280]{2,1,0:T(8,128)(2,1)S(1)}, /*index=5*/s32[]{:T(128)}, s32[]{:T(128)}, s32[]{:T(128)}, s32[]{:T(128)}) while((s32[]{:T(128)}, f32[84,1408]{0,1:T(8,128)S(1)}, s32[]{:T(128)}, bf16[1408,1280]{1,0:T(8,128)(2,1)}, ...), condition=%wide.region_2.3_spmd, body=%wide.region_1.2_spmd.sunk | while | flops 13762566 | bytes 423051 | solution.py:51
  62.4 4.5 %while.41 = (s32[]{:T(128)}, f32[84,1408]{0,1:T(8,128)S(1)}, s32[]{:T(128)}, bf16[1408,1280]{1,0:T(8,128)(2,1)}, bf16[2,84,1280]{2,1,0:T(8,128)(2,1)S(1)}, /*index=5*/s32[]{:T(128)}, s32[]{:T(128)}, s32[]{:T(128)}, s32[]{:T(128)}) while((s32[]{:T(128)}, f32[84,1408]{0,1:T(8,128)S(1)}, s32[]{:T(128)}, bf16[1408,1280]{1,0:T(8,128)(2,1)}, ...), condition=%wide.region_4.5_spmd, body=%wide.region_3.4_spmd.sunk | while | flops 13762566 | bytes 423051 | solution.py:54
  68.6 3.0 %fusion = bf16[16,2816]{1,0:T(8,128)(2,1)S(1)} fusion(bf16[28,2816]{1,0:T(8,128)(2,1)S(1)} %convolution_convert_fusion.3), kind=kCustom, calls=%all-reduce-scatter | all-reduce-scatter fusion | flops 90113 | bytes 248320
  71.6 2.3 %collective-permute-start = (bf16[2,2816]{1,0:T(2,128)(2,1)S(1)}, bf16[2,2816]{1,0:T(2,128)(2,1)S(1)}, u32[]{:S(2)}, u32[]{:S(2)}) collective-permute-start(bf16[2,2816]{1,0:T(2,128)(2,1)S(1)} %slice.52), channel_id=1, source_target_pairs={{0,1},{2,3},{4,5},{6,7},{8,9},{10,11},{12,13},{14,15},{16,17},{18,... | collective-permute-start | bytes 33800
  76.9 3.0 %fusion.1 = bf16[16,2816]{1,0:T(8,128)(2,1)S(1)} fusion(bf16[28,2816]{1,0:T(8,128)(2,1)S(1)} %convolution_convert_fusion.2), kind=kCustom, calls=%all-reduce-scatter.1 | all-reduce-scatter fusion | flops 90113 | bytes 248320
  80.0 2.3 %collective-permute-start.1 = (bf16[2,2816]{1,0:T(2,128)(2,1)S(1)}, bf16[2,2816]{1,0:T(2,128)(2,1)S(1)}, u32[]{:S(2)}, u32[]{:S(2)}) collective-permute-start(bf16[2,2816]{1,0:T(2,128)(2,1)S(1)} %slice.53), channel_id=1, source_target_pairs={{0,1},{2,3},{4,5},{6,7},{8,9},{10,11},{12,13},{14,15},{16,17},{18,... | collective-permute-start | bytes 33800
  86.6 16.7 %all-reduce.7.cloned.1.call-done = bf16[28,2,2816]{2,1,0:T(2,128)(2,1)} async-done(((bf16[28,2,2816]{2,1,0:T(2,128)(2,1)}), bf16[28,2,2816]{2,1,0:T(2,128)(2,1)}) %all-reduce.7.cloned.1.call-update) | async-done | bytes 315408
  105.4 4.9 %while.43 = (s32[]{:T(128)}, f32[84,1280]{1,0:T(8,128)S(1)}, s32[]{:T(128)}, bf16[84,1408]{1,0:T(8,128)(2,1)S(1)}, bf16[1408,1280]{1,0:T(8,128)(2,1)}, /*index=5*/s32[]{:T(128)}, s32[]{:T(128)}, s32[]{:T(128)}, s32[]{:T(128)}) while((s32[]{:T(128)}, f32[84,1280]{1,0:T(8,128)S(1)}, s32[]{:T(128)}, bf16[84,1408]{1,0:T(8,128)(2,1)S(1)}, ...), condition=%wide.region_11.12_spmd, body=%wide.region_10.11_spmd.sunk | while | flops 13870086 | bytes 1068171 | solution.py:77
  106.6 1.2 convolution_add_fusion.5
  109.1 1.2 convolution_add_fusion.5
  110.4 20.7 %while.42 = (s32[]{:T(128)}, f32[84,1280]{1,0:T(8,128)S(1)}, s32[]{:T(128)}, bf16[84,1408]{1,0:T(8,128)(2,1)S(1)}, bf16[1408,1280]{1,0:T(8,128)(2,1)}, /*index=5*/s32[]{:T(128)}, s32[]{:T(128)}, s32[]{:T(128)}, s32[]{:T(128)}) while((s32[]{:T(128)}, f32[84,1280]{1,0:T(8,128)S(1)}, s32[]{:T(128)}, bf16[84,1408]{1,0:T(8,128)(2,1)S(1)}, ...), condition=%wide.region_9.10_spmd, body=%wide.region_8.9_spmd.sunk | while | flops 13870086 | bytes 1068171 | solution.py:76
  110.5 1.2 convolution_add_fusion.4
  111.7 1.2 convolution_add_fusion.4
  112.9 1.2 convolution_add_fusion.4
  114.1 1.2 convolution_add_fusion.4
  115.3 1.2 convolution_add_fusion.4
  117.8 1.2 convolution_add_fusion.4
  120.2 1.2 convolution_add_fusion.4
  121.4 1.2 convolution_add_fusion.4
  122.6 1.2 convolution_add_fusion.4
  123.9 1.2 convolution_add_fusion.4
  125.1 1.2 convolution_add_fusion.4
  127.5 1.2 convolution_add_fusion.4
  129.9 1.2 convolution_add_fusion.4
  131.9 6.4 %copy.98 = bf16[3,14,1280,2,2]{1,4,3,0,2:T(2,128)(2,1)} copy(bf16[3,14,1280,2,2]{2,4,3,1,0:T(2,128)(2,1)S(1)} %maximum_bitcast_fusion) | data formatting | bytes 860160 | tf_op jit(solution)/shard_map/convert_element_type | solution.py:191
  138.3 6.7 %reshape.298 = bf16[16,2,6720]{2,1,0:T(2,128)(2,1)S(1)} reshape(bf16[1280,3,4,14]{3,2,1,0:T(4,128)(2,1)} %bitcast.96) | data formatting | bytes 860160
  145.0 20.5 %all_to_all.33 = bf16[16,2,6720]{2,1,0:T(2,128)(2,1)S(1)} all-to-all(bf16[16,2,6720]{2,1,0:T(2,128)(2,1)S(1)} %reshape.298), channel_id=1, replica_groups=mesh['wave'=16,'lev'=2] {'wave'}, dimensions={0} | all-to-all | bytes 860160 | tf_op jit(solution)/shard_map/all_to_all | solution.py:192
  165.5 10.5 %reshape.299 = bf16[1280,3,4,14]{3,2,1,0:T(4,128)(2,1)} reshape(bf16[16,2,6720]{2,1,0:T(2,128)(2,1)S(1)} %all_to_all.33) | data formatting | bytes 860160
  175.9 5.5 %copy.99 = bf16[3,14,16,80,4]{3,2,4,1,0:T(8,128)(2,1)S(1)} copy(bf16[3,14,16,80,4]{1,4,0,3,2:T(4,128)(2,1)} %bitcast.97) | data formatting | bytes 860160 | tf_op jit(solution)/shard_map/all_to_all | solution.py:192
  (107 shorter events, 49.2 us)
Async XLA Ops:
  7.2 60.9 %copy-start = (f32[28,28]{1,0:T(8,128)S(1)}, f32[28,28]{1,0:T(8,128)}, u32[]{:S(2)}) copy-start(f32[28,28]{1,0:T(8,128)} %param.22) | copy-start | bytes 9412
  7.2 14.3 %copy-start.4 = (s32[16]{0:T(128)S(1)}, s32[16]{0:T(128)}, u32[]{:S(2)}) copy-start(s32[16]{0:T(128)} %param.27) | copy-start | bytes 196
  7.2 18.2 %copy-start.1 = (bf16[3,14,1,2816]{3,1,2,0:T(8,128)(2,1)S(1)}, bf16[3,14,1,2816]{3,1,2,0:T(8,128)(2,1)}, u32[]{:S(2)}) copy-start(bf16[3,14,1,2816]{3,1,2,0:T(8,128)(2,1)} %param.20) | copy-start | bytes 709636
  13.1 28.1 %all-to-all-start = ((bf16[3,14,80,64]{2,1,0,3:T(8,128)(2,1)}), bf16[3,14,80,64]{2,1,0,3:T(8,128)(2,1)S(1)}, u32[]{:S(2)}, u32[]{:S(2)}) async-start(bf16[3,14,80,64]{2,1,0,3:T(8,128)(2,1)} %copy.81), calls=%async_computation | async-start | bytes 1572864 | tf_op jit(solution)/shard_map/all_to_all | solution.py:111
  21.5 81.9 %all-reduce.7.cloned.1.call-start = ((), (), s32[]{:S(2)}) async-start(), calls=%async_computation.2 | async-start | bytes 630784
  67.0 7.6 %copy-start.3 = (u32[32]{0:T(128)S(1)}, u32[32]{0:T(128)}, u32[]{:S(2)}) copy-start(u32[32]{0:T(128)} %constant.117) | copy-start | bytes 388
  67.2 9.2 %copy-start.2 = (f32[28,28]{1,0:T(8,128)S(1)}, f32[28,28]{1,0:T(8,128)}, u32[]{:S(2)}) copy-start(f32[28,28]{1,0:T(8,128)} %param.23) | copy-start | bytes 9412
  67.3 15.0 %copy-start.7 = (f32[28]{0:T(128)S(1)}, f32[28]{0:T(128)}, u32[]{:S(2)}) copy-start(f32[28]{0:T(128)} %param.26) | copy-start | bytes 340
  67.3 16.1 %copy-start.5 = (f32[28,28]{1,0:T(8,128)S(1)}, f32[28,28]{1,0:T(8,128)}, u32[]{:S(2)}) copy-start(f32[28,28]{1,0:T(8,128)} %param.25) | copy-start | bytes 9412
  67.7 16.1 %copy-start.6 = (f32[28,28]{1,0:T(8,128)S(1)}, f32[28,28]{1,0:T(8,128)}, u32[]{:S(2)}) copy-start(f32[28,28]{1,0:T(8,128)} %param.24) | copy-start | bytes 9412
  71.6 4.5 %collective-permute-start = (bf16[2,2816]{1,0:T(2,128)(2,1)S(1)}, bf16[2,2816]{1,0:T(2,128)(2,1)S(1)}, u32[]{:S(2)}, u32[]{:S(2)}) collective-permute-start(bf16[2,2816]{1,0:T(2,128)(2,1)S(1)} %slice.52), channel_id=1, source_target_pairs={{0,1},{2,3},{4,5},{6,7},{8,9},{10,11},{12,13},{14,15},{16,17},{18,... | collective-permute-start | bytes 33800
  80.0 3.1 %collective-permute-start.1 = (bf16[2,2816]{1,0:T(2,128)(2,1)S(1)}, bf16[2,2816]{1,0:T(2,128)(2,1)S(1)}, u32[]{:S(2)}, u32[]{:S(2)}) collective-permute-start(bf16[2,2816]{1,0:T(2,128)(2,1)S(1)} %slice.53), channel_id=1, source_target_pairs={{0,1},{2,3},{4,5},{6,7},{8,9},{10,11},{12,13},{14,15},{16,17},{18,... | collective-permute-start | bytes 33800
Sparse Core Ops, SparseCore 0:
  85.6 17.6 all-reduce.6
where the time goes:
time: 191 us; the launch traced here: 190 us
  matrix products  50.2 us (26%)
  local copies, waits for them, and re-layouts  39.6 us (21%)
  waiting for transfers between devices  33.2 us (17%)
  blocking collectives  26.5 us (14%)
  between operations  19.2 us (10%)
  starting transfers between devices  12.9 us (7%)
  other arithmetic  6.88 us (4%)
    dot_general x21, matrix products, block_step(): jnp.dot(spectra_rows, table_rows, preferred_element_type=jnp.float32)  25 us
    dot_general x21, matrix products, block_step(): lax.dot_general(stacked[which_wave], table_rows, (((1,), (1,)), ((), ()))...  23.2 us
    all_to_all x1, blocking collectives, body(): lax.all_to_all(gridded, 'wave', split_axis=2, concat_axis=3, tiled=True)  20.5 us
    unnamed x24, local copies, waits for them, and re-layouts  19.4 us
    unnamed x4, waiting for transfers between devices  17.5 us
    all_to_all x1, waiting for transfers between devices, body(): lax.all_to_all(masked, 'wave', split_axis=3, concat_axis=2, tiled=True)  15.7 us
    all_to_all x1, starting transfers between devices, body(): lax.all_to_all(masked, 'wave', split_axis=3, concat_axis=2, tiled=True)  8.3 us
    convert_element_type x1, local copies, waits for them, and re-layouts, body(): gridded = grid_part.astype(jnp.bfloat16)  6.42 us
  transfers between devices with their start and end apart: 4, of which 3 were waited for; matrix products, arithmetic and copies ran while one was open for 1% of the time, Pallas kernels for 0%

commit v1 on v0

--- a/solution.py
+++ b/solution.py
@@ -1,3 +1,4 @@
+import functools
 import jax
 import jax.numpy as jnp
 from jax import lax
@@ -7,6 +8,22 @@
 BLOCK = 64
 coupling = 2.0
 highest = lax.Precision.HIGHEST
+
+
+def show_members_all(content, shard_axis, row_dim, pos_dim):
+    e_now = jnp.concatenate(
+        jax.lax.all_to_all(
+            jnp.stack(jnp.split(content, jax.lax.axis_size(shard_axis), axis=row_dim), axis=0),
+            shard_axis,
+            0,
+            0,
+        ),
+        axis=pos_dim,
+    )
+    return e_now
+
+
+surface_solve = functools.partial(show_members_all, shard_axis="wave", row_dim=2, pos_dim=3)
 
 
 def pair_layout(pair_number, row_count):
@@ -189,7 +206,7 @@
         .reshape(3, lev_count, lat_total, 4)
     )
     gridded = grid_part.astype(jnp.bfloat16)
-    returned = lax.all_to_all(gridded, "wave", split_axis=2, concat_axis=3, tiled=True)
+    returned = surface_solve(gridded)
     fourier_out = jnp.where(keep_mask[None, None], returned, jnp.zeros((), jnp.bfloat16))
     return (spectral_new, fourier_out)
 

time: 191 us -> 170 us (0.89)
  local copies, waits for them, and re-layouts: 39.6 us -> 12.4 us
  blocking collectives: 26.5 us -> 32.4 us
    unnamed x24 -> x34, local copies, waits for them, and re-layouts: 19.4 us -> 4.72 us
    convert_element_type x1, local copies, waits for them, and re-layouts: 6.42 us -> 0.17 us  [body(): gridded = grid_part.astype(jnp.bfloat16)]
    all_to_all x1, blocking collectives: 20.5 us -> 26.5 us  [show_members_all(): jax.lax.all_to_all(jnp.stack(jnp.split(content, jax.lax.axis_size(shard_a...]
    all_to_all x2 -> x0, local copies, waits for them, and re-layouts: 5.79 us -> none  [body(): lax.all_to_all(gridded, 'wave', split_axis=2, concat_axis=3, tiled=True)]
  transfers between devices with their start and end apart: 4 -> 4, of which waited for: 3 -> 3; matrix products, arithmetic and copies ran while one was open for 1% -> 3% of each run, Pallas kernels for 0% -> 0%
where the time goes in v1:
time: 170 us; the launch traced here: 168 us
  matrix products  50.2 us (30%)
  blocking collectives  32.4 us (19%)
  waiting for transfers between devices  31.6 us (19%)
  between operations  19.2 us (11%)
  starting transfers between devices  12.9 us (8%)
  local copies, waits for them, and re-layouts  12.4 us (7%)
  other arithmetic  8.29 us (5%)
    all_to_all x1, blocking collectives, show_members_all(): jax.lax.all_to_all(jnp.stack(jnp.split(content, jax.lax.axis_size(shard_a...  26.5 us
    dot_general x21, matrix products, block_step(): jnp.dot(spectra_rows, table_rows, preferred_element_type=jnp.float32)  25 us
    dot_general x21, matrix products, block_step(): lax.dot_general(stacked[which_wave], table_rows, (((1,), (1,)), ((), ()))...  23.2 us
    unnamed x4, waiting for transfers between devices  17.5 us
    all_to_all x1, waiting for transfers between devices, body(): lax.all_to_all(masked, 'wave', split_axis=3, concat_axis=2, tiled=True)  14.1 us
    all_to_all x1, starting transfers between devices, body(): lax.all_to_all(masked, 'wave', split_axis=3, concat_axis=2, tiled=True)  8.3 us
    unnamed x2, blocking collectives  5.99 us
    unnamed x34, local copies, waits for them, and re-layouts  4.72 us
  transfers between devices with their start and end apart: 4, of which 3 were waited for; matrix products, arithmetic and copies ran while one was open for 3% of the time, Pallas kernels for 0%

profile of v1, /device:TPU:0, one launch (start us, length us, event | category | flops | bytes accessed | tf_op | source)
XLA Modules:
  0.0 168.3 jit_solution(2551574165118036272)
XLA Ops:
  10.6 2.4 %copy_select_fusion = bf16[3,14,80,64]{2,1,0,3:T(8,128)(2,1)} fusion(bf16[3,14,80,64]{2,3,1,0:T(8,128)(2,1)} %param.19, pred[80,64]{0,1:T(8,128)(4,1)S(1)} %broadcast_compare_fusion), kind=kLoop, calls=%fused_computation.27 | loop fusion | flops 215040 | bytes 865280 | tf_op jit(solution)/shard_map/jit(_where)/select_n | solution.py:127
  13.0 8.3 %all-to-all-start = ((bf16[3,14,80,64]{2,1,0,3:T(8,128)(2,1)}), bf16[3,14,80,64]{2,1,0,3:T(8,128)(2,1)S(1)}, u32[]{:S(2)}, u32[]{:S(2)}) async-start(bf16[3,14,80,64]{2,1,0,3:T(8,128)(2,1)} %copy_select_fusion), calls=%async_computation | async-start | bytes 1572864 | tf_op jit(solution)/shard_map/all_to_all | solution.py:128
  21.4 1.2 dynamic_slice.39
  26.9 14.1 %all-to-all-done = bf16[3,14,80,64]{2,1,0,3:T(8,128)(2,1)S(1)} async-done(((bf16[3,14,80,64]{2,1,0,3:T(8,128)(2,1)}), bf16[3,14,80,64]{2,1,0,3:T(8,128)(2,1)S(1)}, u32[]{:S(2)}, u32[]{:S(2)}) %all-to-all-start) | async-done | bytes 430112 | tf_op jit(solution)/shard_map/all_to_all | solution.py:128
  43.0 19.3 %while.40 = (s32[]{:T(128)}, f32[84,1408]{0,1:T(8,128)S(1)}, s32[]{:T(128)}, bf16[1408,1280]{1,0:T(8,128)(2,1)}, bf16[2,84,1280]{2,1,0:T(8,128)(2,1)S(1)}, /*index=5*/s32[]{:T(128)}, s32[]{:T(128)}, s32[]{:T(128)}, s32[]{:T(128)}) while((s32[]{:T(128)}, f32[84,1408]{0,1:T(8,128)S(1)}, s32[]{:T(128)}, bf16[1408,1280]{1,0:T(8,128)(2,1)}, ...), condition=%wide.region_2.3_spmd, body=%wide.region_1.2_spmd.sunk | while | flops 13762566 | bytes 423051 | solution.py:68
  62.4 4.5 %while.41 = (s32[]{:T(128)}, f32[84,1408]{0,1:T(8,128)S(1)}, s32[]{:T(128)}, bf16[1408,1280]{1,0:T(8,128)(2,1)}, bf16[2,84,1280]{2,1,0:T(8,128)(2,1)S(1)}, /*index=5*/s32[]{:T(128)}, s32[]{:T(128)}, s32[]{:T(128)}, s32[]{:T(128)}) while((s32[]{:T(128)}, f32[84,1408]{0,1:T(8,128)S(1)}, s32[]{:T(128)}, bf16[1408,1280]{1,0:T(8,128)(2,1)}, ...), condition=%wide.region_4.5_spmd, body=%wide.region_3.4_spmd.sunk | while | flops 13762566 | bytes 423051 | solution.py:71
  68.5 3.0 %fusion = bf16[16,2816]{1,0:T(8,128)(2,1)S(1)} fusion(bf16[28,2816]{1,0:T(8,128)(2,1)S(1)} %convolution_convert_fusion.3), kind=kCustom, calls=%all-reduce-scatter | all-reduce-scatter fusion | flops 90113 | bytes 248320
  71.5 2.3 %collective-permute-start = (bf16[2,2816]{1,0:T(2,128)(2,1)S(1)}, bf16[2,2816]{1,0:T(2,128)(2,1)S(1)}, u32[]{:S(2)}, u32[]{:S(2)}) collective-permute-start(bf16[2,2816]{1,0:T(2,128)(2,1)S(1)} %slice.52), channel_id=1, source_target_pairs={{0,1},{2,3},{4,5},{6,7},{8,9},{10,11},{12,13},{14,15},{16,17},{18,... | collective-permute-start | bytes 33800
  76.9 3.0 %fusion.1 = bf16[16,2816]{1,0:T(8,128)(2,1)S(1)} fusion(bf16[28,2816]{1,0:T(8,128)(2,1)S(1)} %convolution_convert_fusion.2), kind=kCustom, calls=%all-reduce-scatter.1 | all-reduce-scatter fusion | flops 90113 | bytes 248320
  79.9 2.3 %collective-permute-start.1 = (bf16[2,2816]{1,0:T(2,128)(2,1)S(1)}, bf16[2,2816]{1,0:T(2,128)(2,1)S(1)}, u32[]{:S(2)}, u32[]{:S(2)}) collective-permute-start(bf16[2,2816]{1,0:T(2,128)(2,1)S(1)} %slice.53), channel_id=1, source_target_pairs={{0,1},{2,3},{4,5},{6,7},{8,9},{10,11},{12,13},{14,15},{16,17},{18,... | collective-permute-start | bytes 33800
  86.5 16.8 %all-reduce.7.cloned.1.call-done = bf16[28,2,2816]{2,1,0:T(2,128)(2,1)} async-done(((bf16[28,2,2816]{2,1,0:T(2,128)(2,1)}), bf16[28,2,2816]{2,1,0:T(2,128)(2,1)}) %all-reduce.7.cloned.1.call-update) | async-done | bytes 315408
  105.3 20.8 %while.42 = (s32[]{:T(128)}, f32[84,1280]{1,0:T(8,128)S(1)}, s32[]{:T(128)}, bf16[84,1408]{1,0:T(8,128)(2,1)S(1)}, bf16[1408,1280]{1,0:T(8,128)(2,1)}, /*index=5*/s32[]{:T(128)}, s32[]{:T(128)}, s32[]{:T(128)}, s32[]{:T(128)}) while((s32[]{:T(128)}, f32[84,1280]{1,0:T(8,128)S(1)}, s32[]{:T(128)}, bf16[84,1408]{1,0:T(8,128)(2,1)S(1)}, ...), condition=%wide.region_9.10_spmd, body=%wide.region_8.9_spmd.sunk | while | flops 13870086 | bytes 1068171 | solution.py:93
  106.6 1.2 convolution_add_fusion.4
  107.8 1.2 convolution_add_fusion.4
  109.0 1.2 convolution_add_fusion.4
  110.2 1.2 convolution_add_fusion.4
  111.4 1.2 convolution_add_fusion.4
  112.7 1.2 convolution_add_fusion.4
  113.9 1.2 convolution_add_fusion.4
  115.1 1.2 convolution_add_fusion.4
  116.3 1.2 convolution_add_fusion.4
  117.5 1.2 convolution_add_fusion.4
  118.8 1.2 convolution_add_fusion.4
  120.0 1.2 convolution_add_fusion.4
  121.2 1.2 convolution_add_fusion.4
  122.4 1.2 convolution_add_fusion.4
  123.6 1.2 convolution_add_fusion.4
  124.9 1.2 convolution_add_fusion.4
  126.3 4.9 %while.43 = (s32[]{:T(128)}, f32[84,1280]{1,0:T(8,128)S(1)}, s32[]{:T(128)}, bf16[84,1408]{1,0:T(8,128)(2,1)S(1)}, bf16[1408,1280]{1,0:T(8,128)(2,1)}, /*index=5*/s32[]{:T(128)}, s32[]{:T(128)}, s32[]{:T(128)}, s32[]{:T(128)}) while((s32[]{:T(128)}, f32[84,1280]{1,0:T(8,128)S(1)}, s32[]{:T(128)}, bf16[84,1408]{1,0:T(8,128)(2,1)S(1)}, ...), condition=%wide.region_11.12_spmd, body=%wide.region_10.11_spmd.sunk | while | flops 13870086 | bytes 1068171 | solution.py:94
  126.3 1.2 convolution_add_fusion.5
  127.5 1.2 convolution_add_fusion.5
  133.7 26.5 %all_to_all.20 = bf16[16,3,14,80,4]{3,4,2,1,0:T(4,128)(2,1)S(1)} all-to-all(bf16[16,3,14,80,4]{3,4,2,1,0:T(4,128)(2,1)S(1)} %fusion.45), channel_id=1, replica_groups=mesh['wave'=16,'lev'=2] {'wave'}, dimensions={0} | all-to-all | bytes 860160 | tf_op jit(solution)/shard_map/all_to_all | solution.py:15
  (116 shorter events, 46.6 us)
Async XLA Ops:
  7.2 60.8 %copy-start = (f32[28,28]{1,0:T(8,128)S(1)}, f32[28,28]{1,0:T(8,128)}, u32[]{:S(2)}) copy-start(f32[28,28]{1,0:T(8,128)} %param.22) | copy-start | bytes 9412
  13.0 28.1 %all-to-all-start = ((bf16[3,14,80,64]{2,1,0,3:T(8,128)(2,1)}), bf16[3,14,80,64]{2,1,0,3:T(8,128)(2,1)S(1)}, u32[]{:S(2)}, u32[]{:S(2)}) async-start(bf16[3,14,80,64]{2,1,0,3:T(8,128)(2,1)} %copy_select_fusion), calls=%async_computation | async-start | bytes 1572864 | tf_op jit(solution)/shard_map/all_to_all | solution.py:128
  21.3 81.9 %all-reduce.7.cloned.1.call-start = ((), (), s32[]{:S(2)}) async-start(), calls=%async_computation.2 | async-start | bytes 630784
  67.2 7.3 %copy-start.2 = (u32[32]{0:T(128)S(1)}, u32[32]{0:T(128)}, u32[]{:S(2)}) copy-start(u32[32]{0:T(128)} %constant.117) | copy-start | bytes 388
  67.2 9.2 %copy-start.1 = (f32[28,28]{1,0:T(8,128)S(1)}, f32[28,28]{1,0:T(8,128)}, u32[]{:S(2)}) copy-start(f32[28,28]{1,0:T(8,128)} %param.23) | copy-start | bytes 9412
  67.2 15.0 %copy-start.5 = (f32[28]{0:T(128)S(1)}, f32[28]{0:T(128)}, u32[]{:S(2)}) copy-start(f32[28]{0:T(128)} %param.26) | copy-start | bytes 340
  67.2 16.0 %copy-start.3 = (f32[28,28]{1,0:T(8,128)S(1)}, f32[28,28]{1,0:T(8,128)}, u32[]{:S(2)}) copy-start(f32[28,28]{1,0:T(8,128)} %param.24) | copy-start | bytes 9412
  67.7 16.1 %copy-start.4 = (f32[28,28]{1,0:T(8,128)S(1)}, f32[28,28]{1,0:T(8,128)}, u32[]{:S(2)}) copy-start(f32[28,28]{1,0:T(8,128)} %param.25) | copy-start | bytes 9412
  71.5 4.6 %collective-permute-start = (bf16[2,2816]{1,0:T(2,128)(2,1)S(1)}, bf16[2,2816]{1,0:T(2,128)(2,1)S(1)}, u32[]{:S(2)}, u32[]{:S(2)}) collective-permute-start(bf16[2,2816]{1,0:T(2,128)(2,1)S(1)} %slice.52), channel_id=1, source_target_pairs={{0,1},{2,3},{4,5},{6,7},{8,9},{10,11},{12,13},{14,15},{16,17},{18,... | collective-permute-start | bytes 33800
  79.9 3.1 %collective-permute-start.1 = (bf16[2,2816]{1,0:T(2,128)(2,1)S(1)}, bf16[2,2816]{1,0:T(2,128)(2,1)S(1)}, u32[]{:S(2)}, u32[]{:S(2)}) collective-permute-start(bf16[2,2816]{1,0:T(2,128)(2,1)S(1)} %slice.53), channel_id=1, source_target_pairs={{0,1},{2,3},{4,5},{6,7},{8,9},{10,11},{12,13},{14,15},{16,17},{18,... | collective-permute-start | bytes 33800
Sparse Core Ops, SparseCore 0:
  85.5 17.6 all-reduce.6
